TPU v7x, 32 devices: a whole 2x2x4 slice. The times are simulated.
32 devices in a mesh: groups: 2 (over y), inp: 2 (over x), outp: 4 (over z), depth: 2 (over core).
Axes of the slice: x: 2, y: 2, z: 4, core: 2. Of those that a mesh axis runs over, the one named last changes fastest.
Arguments:
- tokens: bfloat16 [1024, 5120], P(('groups', 'depth', 'outp'), 'inp'), parts along dimension 0, may hold values from -6 to 6
- gate_pre: bfloat16 [1024, 16384], P(('groups', 'depth', 'inp'), 'outp'), parts along dimension 0, may hold values from -8 to 8
- up_pre: bfloat16 [1024, 16384], P(('groups', 'depth', 'inp'), 'outp'), parts along dimension 0, may hold values from -6 to 6
- grad_hidden: bfloat16 [1024, 16384], P(('groups', 'depth', 'inp'), 'outp'), parts along dimension 0, may hold values from -2.109375 to 2.109375
- gate_weight: bfloat16 [5120, 16384], P('inp', ('outp', 'depth')), may hold values from -0.078125 to 0.078125
- up_weight: bfloat16 [5120, 16384], P('inp', ('outp', 'depth')), may hold values from -0.078125 to 0.078125
Outputs:
- grad_tokens: bfloat16 [1024, 5120], P(('groups', 'depth', 'outp'), 'inp'), parts along dimension 0
- grad_gate_weight: bfloat16 [10240, 16384], P(('groups', 'inp'), ('outp', 'depth')), parts along dimension 0
- grad_up_weight: bfloat16 [10240, 16384], P(('groups', 'inp'), ('outp', 'depth')), parts along dimension 0
There are 2 independent parts, one for each index of `groups`. A program takes and returns all parts, laid end to end along the dimension named above; an argument that names none is the same for every part. Nothing has to cross between parts.
All inputs are finite; a program needn't handle non-finite values.
Results may differ from a plain program's by a relative error of at most 0.0059.
Values may be sent and summed in bfloat16 or wider, within the bound.
A program may use at most 256 MiB of HBM per device.

v0:
```python
import jax
import jax.numpy as jnp
from jax import lax
from jax.sharding import PartitionSpec as P


def rows_product(left, right):
    return lax.dot_general(
        left, right, (((0,), (0,)), ((), ())), preferred_element_type=jnp.float32
    )


def cols_product(left, right):
    return lax.dot_general(
        left, right, (((1,), (1,)), ((), ())), preferred_element_type=jnp.float32
    )


def local(tokens, gate_pre, up_pre, grad_hidden, gate_weight, up_weight):
    g = gate_pre.astype(jnp.float32)
    u = up_pre.astype(jnp.float32)
    h = grad_hidden.astype(jnp.float32)
    s = jax.nn.sigmoid(g)
    grad_up = (h * g * s).astype(jnp.bfloat16)
    grad_gate = (h * u * s * (1.0 + g * (1.0 - s))).astype(jnp.bfloat16)
    panel_gate, panel_up = (
        lax.all_gather(grad_gate, "inp", axis=0, tiled=True),
        lax.all_gather(grad_up, "inp", axis=0, tiled=True),
    )
    local_rows = lax.all_gather(tokens, "outp", axis=0, tiled=True)
    full_gate, full_up = (
        lax.all_gather(gate_weight, "depth", axis=1, tiled=True),
        lax.all_gather(up_weight, "depth", axis=1, tiled=True),
    )
    grad_tokens = lax.psum_scatter(
        cols_product(panel_gate, full_gate) + cols_product(panel_up, full_up),
        "outp",
        scatter_dimension=0,
        tiled=True,
    )
    weight_gate = rows_product(local_rows, panel_gate)
    weight_up = rows_product(local_rows, panel_up)
    sum_gate, sum_up = (
        lax.psum_scatter(
            weight_gate.astype(jnp.bfloat16), "depth", scatter_dimension=1, tiled=True
        ).astype(jnp.float32),
        lax.psum_scatter(
            weight_up.astype(jnp.bfloat16), "depth", scatter_dimension=1, tiled=True
        ).astype(jnp.float32),
    )
    out_gate = sum_gate.astype(jnp.bfloat16)
    out_up = sum_up.astype(jnp.bfloat16)
    return (grad_tokens.astype(jnp.bfloat16), out_gate, out_up)


def solution(mesh):
    placed = (
        P(("groups", "depth", "outp"), "inp"),
        P(("groups", "depth", "inp"), "outp"),
        P(("groups", "depth", "inp"), "outp"),
        P(("groups", "depth", "inp"), "outp"),
        P("inp", ("outp", "depth")),
        P("inp", ("outp", "depth")),
    )
    return jax.shard_map(
        local,
        mesh=mesh,
        in_specs=placed,
        out_specs=(
            P(("groups", "depth", "outp"), "inp"),
            P(("groups", "inp"), ("outp", "depth")),
            P(("groups", "inp"), ("outp", "depth")),
        ),
        check_vma=False,
    )
```

profile of v0, /device:TPU:0, one launch (start us, length us, event | category | flops | bytes accessed | tf_op | source)
XLA Modules:
  0.0 336.0 jit_solution(7230607341345219336)
XLA Ops:
  7.2 4.3 %fusion.10 = (bf16[128,4096]{1,0:T(8,128)(2,1)}, bf16[128,4096]{1,0:T(8,128)(2,1)}) fusion(bf16[128,4096]{1,0:T(8,128)(2,1)} %param.7, bf16[128,4096]{1,0:T(8,128)(2,1)} %param.9, bf16[128,4096]{1,0:T(8,128)(2,1)} %param.8), kind=kLoop, calls=%fused_computation.17 | loop fusion | flops 8388608 | bytes 5242880 | tf_op jit(solution)/shard_map/convert_element_type | solution.py:24
  11.5 0.7 all-gather.8.cloned.1.call-update
  12.3 0.7 all-gather.10.cloned.1.call-update
  13.0 0.5 all-gather.12.cloned.1.call-update
  13.6 0.5 all-gather.14.cloned.1.call-update
  14.2 33.3 %all-gather.6.cloned.1.call-done = bf16[256,4096]{1,0:T(8,128)(2,1)} async-done(((bf16[128,4096]{1,0:T(8,128)(2,1)}), bf16[256,4096]{1,0:T(8,128)(2,1)}) %all-gather.6.cloned.1.call-update) | async-done | bytes 2097168 | tf_op jit(solution)/shard_map/all_gather | solution.py:27
  47.5 37.5 %all-gather.8.cloned.1.call-done = bf16[2560,4096]{1,0:T(8,128)(2,1)} async-done(((bf16[2560,2048]{1,0:T(8,128)(2,1)}), bf16[2560,4096]{1,0:T(8,128)(2,1)}) %all-gather.8.cloned.1.call-update) | async-done | bytes 20971536 | tf_op jit(solution)/shard_map/all_gather | solution.py:32
  84.9 10.5 %fusion.11 = f32[256,2560]{1,0:T(8,128)S(1)} fusion(bf16[256,4096]{1,0:T(8,128)(2,1)} %all-gather.6.cloned.1.call-done, bf16[2560,4096]{1,0:T(8,128)(2,1)} %all-gather.8.cloned.1.call-done), kind=kOutput, calls=%fused_computation.18 | convolution fusion | flops 5368709120 | bytes 25690112 | tf_op jit(solution)/shard_map/dot_general | solution.py:14
  95.4 25.9 %all-gather.10.cloned.1.call-done = bf16[256,4096]{1,0:T(8,128)(2,1)} async-done(((bf16[128,4096]{1,0:T(8,128)(2,1)}), bf16[256,4096]{1,0:T(8,128)(2,1)}) %all-gather.10.cloned.1.call-update) | async-done | bytes 2097168 | tf_op jit(solution)/shard_map/all_gather | solution.py:28
  121.4 37.3 %all-gather.12.cloned.1.call-done = bf16[2560,4096]{1,0:T(8,128)(2,1)} async-done(((bf16[2560,2048]{1,0:T(8,128)(2,1)}), bf16[2560,4096]{1,0:T(8,128)(2,1)}) %all-gather.12.cloned.1.call-update) | async-done | bytes 20971536 | tf_op jit(solution)/shard_map/all_gather | solution.py:33
  158.7 11.6 %convolution_add_fusion = f32[256,2560]{1,0:T(8,128)} fusion(f32[256,2560]{1,0:T(8,128)S(1)} %fusion.11, bf16[256,4096]{1,0:T(8,128)(2,1)} %all-gather.10.cloned.1.call-done, bf16[2560,4096]{1,0:T(8,128)(2,1)} %all-gather.12.cloned.1.call-done), kind=kOutput, calls=%fused_computation.4 | convolution fusion | flops 5369364480 | bytes 28311552 | tf_op jit(solution)/shard_map/dot_general | solution.py:14
  170.3 0.0 reduce-scatter.12.cloned.1.call-start
  170.3 23.7 %all-gather.14.cloned.1.call-done = bf16[256,2560]{1,0:T(8,128)(2,1)} async-done(((bf16[64,2560]{1,0:T(8,128)(2,1)}), bf16[256,2560]{1,0:T(8,128)(2,1)}) %all-gather.14.cloned.1.call-update) | async-done | bytes 1310736 | tf_op jit(solution)/shard_map/all_gather | solution.py:30
  194.0 11.5 %fusion = bf16[2560,4096]{0,1:T(8,128)(2,1)} fusion(bf16[256,4096]{1,0:T(8,128)(2,1)S(1)} %copy-done.1, bf16[256,2560]{1,0:T(8,128)(2,1)} %all-gather.14.cloned.1.call-done), kind=kOutput, calls=%fused_computation.2 | convolution fusion | flops 5379194880 | bytes 24379392 | tf_op jit(solution)/shard_map/dot_general | solution.py:8
  205.6 0.2 reduce-scatter.14.cloned.1.call-start
  205.8 1.1 copy-done
  206.8 0.7 copy-done.2
  207.5 10.0 %fusion.1 = bf16[2560,4096]{0,1:T(8,128)(2,1)} fusion(bf16[256,4096]{1,0:T(8,128)(2,1)S(1)} %copy-done.2, bf16[256,2560]{1,0:T(8,128)(2,1)S(1)} %copy-done), kind=kOutput, calls=%fused_computation.3 | convolution fusion | flops 5379194880 | bytes 24379392 | tf_op jit(solution)/shard_map/dot_general | solution.py:8
  217.5 30.3 %reduce-scatter.10.cloned.1.call-done = f32[64,2560]{1,0:T(8,128)} async-done(((f32[256,2560]{1,0:T(8,128)}), f32[64,2560]{1,0:T(8,128)}) %reduce-scatter.10.cloned.1.call-update) | async-done | bytes 655376 | tf_op jit(solution)/shard_map/reduce_scatter | solution.py:35
  247.9 1.8 convert_element_type.39
  249.7 30.8 %reduce-scatter.12.cloned.1.call-done = bf16[2560,2048]{0,1:T(8,128)(2,1)} async-done(((bf16[2560,4096]{0,1:T(8,128)(2,1)}), bf16[2560,2048]{0,1:T(8,128)(2,1)}) %reduce-scatter.12.cloned.1.call-update) | async-done | bytes 10485776
  280.5 14.7 %copy.11 = bf16[2560,2048]{1,0:T(8,128)(2,1)} copy(bf16[2560,2048]{0,1:T(8,128)(2,1)} %reduce-scatter.12.cloned.1.call-done) | data formatting | bytes 20971520
  295.2 19.6 %reduce-scatter.14.cloned.1.call-done = bf16[2560,2048]{0,1:T(8,128)(2,1)} async-done(((bf16[2560,4096]{0,1:T(8,128)(2,1)}), bf16[2560,2048]{0,1:T(8,128)(2,1)}) %reduce-scatter.14.cloned.1.call-update) | async-done | bytes 10485776
  314.8 14.4 %copy.12 = bf16[2560,2048]{1,0:T(8,128)(2,1)} copy(bf16[2560,2048]{0,1:T(8,128)(2,1)} %reduce-scatter.14.cloned.1.call-done) | data formatting | bytes 20971520
  (14 shorter events, 0.3 us)
Async XLA Ops:
  7.2 40.3 %all-gather.6.cloned.1.call-start = ((), (), s32[]{:S(2)}) async-start(), calls=%async_computation.3 | async-start | bytes 3145728 | tf_op jit(solution)/shard_map/all_gather | solution.py:27
  11.5 73.4 %all-gather.8.cloned.1.call-start = ((), (), s32[]{:S(2)}) async-start(), calls=%async_computation.4 | async-start | bytes 31457280 | tf_op jit(solution)/shard_map/all_gather | solution.py:32
  12.3 109.1 %all-gather.10.cloned.1.call-start = ((), (), s32[]{:S(2)}) async-start(), calls=%async_computation.5 | async-start | bytes 3145728 | tf_op jit(solution)/shard_map/all_gather | solution.py:28
  13.0 145.7 %all-gather.12.cloned.1.call-start = ((), (), s32[]{:S(2)}) async-start(), calls=%async_computation.6 | async-start | bytes 31457280 | tf_op jit(solution)/shard_map/all_gather | solution.py:33
  13.6 180.4 %all-gather.14.cloned.1.call-start = ((), (), s32[]{:S(2)}) async-start(), calls=%async_computation.8 | async-start | bytes 1638400 | tf_op jit(solution)/shard_map/all_gather | solution.py:30
  14.2 233.7 %reduce-scatter.10.cloned.1.call-start = ((), (), s32[]{:S(2)}) async-start(), calls=%async_computation.7 | async-start | bytes 3276800 | tf_op jit(solution)/shard_map/reduce_scatter | solution.py:35
  170.2 23.8 %copy-start.1 = (bf16[256,4096]{1,0:T(8,128)(2,1)S(1)}, bf16[256,4096]{1,0:T(8,128)(2,1)}, u32[]{:S(2)}) copy-start(bf16[256,4096]{1,0:T(8,128)(2,1)} %all-gather.6.cloned.1.call-done) | copy-start | bytes 6291460
  170.3 110.3 %reduce-scatter.12.cloned.1.call-start = ((), (), s32[]{:S(2)}) async-start(), calls=%async_computation.9 | async-start | bytes 31457280
  205.5 1.3 copy-start
  205.5 2.0 copy-start.2
  205.6 109.2 %reduce-scatter.14.cloned.1.call-start = ((), (), s32[]{:S(2)}) async-start(), calls=%async_computation.10 | async-start | bytes 31457280
Sparse Core Ops, SparseCore 0:
  11.6 35.8 all-gather.5
  49.0 35.8 all-gather.7
  87.1 34.2 all-gather.9
  122.8 35.8 all-gather.11
  160.1 33.8 all-gather.13
  196.7 51.0 reduce-scatter.9
  250.2 30.3 reduce-scatter.11
  282.8 31.8 reduce-scatter.13
where the time goes:
time: 337 us; the launch traced here: 336 us
  waiting for transfers between devices  241 us (72%)
  matrix products  43.5 us (13%)
  local copies, waits for them, and re-layouts  30.8 us (9%)
  between operations  14.1 us (4%)
  other arithmetic  6.11 us (2%)
    unnamed x10, waiting for transfers between devices  52.9 us
    all_gather x1, waiting for transfers between devices, local(): lax.all_gather(gate_weight, 'depth', axis=1, tiled=True)  37.5 us
    all_gather x1, waiting for transfers between devices, local(): lax.all_gather(up_weight, 'depth', axis=1, tiled=True)  37.3 us
    all_gather x1, waiting for transfers between devices, local(): lax.all_gather(grad_gate, 'inp', axis=0, tiled=True)  33.3 us
    unnamed x8, local copies, waits for them, and re-layouts  30.8 us
    reduce_scatter x1, waiting for transfers between devices, local(): lax.psum_scatter(cols_product(panel_gate, full_gate) + cols_product(panel...  30.3 us
    all_gather x1, waiting for transfers between devices, local(): lax.all_gather(grad_up, 'inp', axis=0, tiled=True)  25.9 us
    all_gather x1, waiting for transfers between devices, local(): local_rows = lax.all_gather(tokens, 'outp', axis=0, tiled=True)  23.7 us
  transfers between devices with their start and end apart: 8, of which 8 were waited for; matrix products, arithmetic and copies ran while one was open for 18% of the time, Pallas kernels for 0%

commit v1 on v0

v1 whole, which is shorter than its diff:
```python
import functools

import jax
import jax.numpy as jnp
from jax import lax
from jax.experimental import pallas as pl
from jax.experimental.pallas import tpu as pltpu
from jax.sharding import PartitionSpec as P

MESH = pl.DeviceIdType.MESH
f32, bf16 = jnp.float32, jnp.bfloat16
VMEM_BYTES = 60 * 1024 * 1024


def width(extent):
    return 256 if extent % 256 == 0 else 128


def exchange(
    n_inp, n_outp,
    tokens, gate, up, hidden, w_gate, w_up,
    out, grads_out, turned_out,
    gv, uv, hv, wg, wu, tk, turned, gr, sb, pf, pb, xr, zs, zr, ov,
    in_sem, own_sem, w_sem, t_send, t_recv, f_send, f_recv,
    g_send, g_recv, x_send, x_recv, z_send, z_recv, o_sem, out_sem,
):
    i, o, d = lax.axis_index("inp"), lax.axis_index("outp"), lax.axis_index("depth")
    e = 1 - d
    rows, feats = tokens.shape
    per = gate.shape[0] // rows
    half = gate.shape[1] // 2
    inps = [lax.rem(i + s, n_inp) for s in range(n_inp)]
    outps = [lax.rem(o + s, n_outp) for s in range(n_outp)]

    loads = []
    for p in range(per):
        part = pl.ds(p * rows, rows)
        loads.append([
            pltpu.make_async_copy(src.at[part], dst.at[part], in_sem.at[p, k])
            for k, (src, dst) in enumerate(((gate, gv), (up, uv), (hidden, hv)))
        ])
    own = pltpu.make_async_copy(tokens, tk.at[o, d], own_sem)
    weights = [
        pltpu.make_async_copy(w_gate, wg, w_sem.at[0]),
        pltpu.make_async_copy(w_up, wu, w_sem.at[1]),
    ]
    for copy in loads[0] + [own] + sum(loads[1:], []) + weights:
        copy.start()

    barrier = pltpu.get_barrier_semaphore()
    for s in range(n_inp):
        for q in ((e,) if s == 0 else (d, e)):
            pl.semaphore_signal(barrier, inc=1, device_id={"inp": inps[s], "depth": q}, device_id_type=MESH)
    for s in range(1, n_outp):
        pl.semaphore_signal(barrier, inc=1, device_id={"outp": outps[s]}, device_id_type=MESH)
    pl.semaphore_wait(barrier, 2 * n_inp - 1 + n_outp - 1)

    cw = width(half)

    def pointwise(p, side, store):
        def step(c, carry):
            at = (pl.ds(p * rows, rows), pl.ds(pl.multiple_of(side * half + c * cw, cw), cw))
            g, u, h = gv[at].astype(f32), uv[at].astype(f32), hv[at].astype(f32)
            sig = 1.0 / (1.0 + jnp.exp(-g))
            hs = h * sig
            cols = pl.ds(pl.multiple_of(c * cw, cw), cw)
            store(cols, (hs * u * (1.0 + g * (1.0 - sig))).astype(bf16), (hs * g).astype(bf16))
            return carry
        lax.fori_loop(0, half // cw, step, 0)

    def grad_copy(p, s, q, src):
        slot = gr.at[:, i * per + p, d]
        return pltpu.make_async_remote_copy(
            src_ref=src, dst_ref=slot,
            send_sem=g_send.at[s, q, p], recv_sem=g_recv.at[i, d, p],
            device_id={"inp": inps[s], "depth": d if q == 0 else e}, device_id_type=MESH,
        )

    sends = []
    for p in range(per):
        for copy in loads[p]:
            copy.wait()
        mine = i * per + p

        def store_there(cols, a, b):
            sb[0, p, :, cols] = a
            sb[1, p, :, cols] = b

        def store_here(cols, a, b):
            gr[0, mine, d, :, cols] = a
            gr[1, mine, d, :, cols] = b

        pointwise(p, e, store_there)
        for s in list(range(1, n_inp)) + [0]:
            copy = grad_copy(p, s, 1, sb.at[:, p])
            copy.start()
            sends.append(copy)
        pointwise(p, d, store_here)
        for s in range(1, n_inp):
            copy = grad_copy(p, s, 0, gr.at[:, mine, d])
            copy.start()
            sends.append(copy)
        if p == 0:
            own.wait()
            for s in range(1, n_outp):
                copy = pltpu.make_async_remote_copy(
                    src_ref=tk.at[o, d], dst_ref=tk.at[o, d],
                    send_sem=t_send.at[s], recv_sem=t_recv.at[o],
                    device_id={"outp": outps[s]}, device_id_type=MESH,
                )
                copy.start()
                sends.append(copy)

    def await_grads(j, q, p):
        slot = gr.at[:, j * per + p, q]
        pltpu.make_async_remote_copy(
            src_ref=slot, dst_ref=slot, send_sem=g_send.at[0, 0, 0], recv_sem=g_recv.at[j, q, p],
            device_id={"depth": e}, device_id_type=MESH,
        ).wait_recv()

    fw = width(feats)

    def product(c):
        left_gate = gr[0, c].reshape(2 * rows, half)
        left_up = gr[1, c].reshape(2 * rows, half)

        def step(t, carry):
            cols = pl.ds(pl.multiple_of(t * fw, fw), fw)
            contract = (((1,), (1,)), ((), ()))
            acc = lax.dot_general(left_gate, wg[cols, :], contract, preferred_element_type=f32)
            acc = acc + lax.dot_general(left_up, wu[cols, :], contract, preferred_element_type=f32)
            acc = acc.reshape(2, rows, fw)
            pf[c, :, :, cols] = acc
            pb[c, :, :, cols] = acc.astype(bf16)
            return carry
        lax.fori_loop(0, feats // fw, step, 0)

    def pair_copy(c):
        return pltpu.make_async_remote_copy(
            src_ref=pb.at[c, e], dst_ref=xr.at[c], send_sem=x_send.at[c], recv_sem=x_recv.at[c],
            device_id={"depth": e}, device_id_type=MESH,
        )

    def store_grads(c):
        return pltpu.make_async_copy(gr.at[:, c], grads_out.at[:, c], o_sem.at[c])

    def spread_copy(c):
        return pltpu.make_async_remote_copy(
            src_ref=zs.at[c], dst_ref=zr.at[o], send_sem=z_send.at[c], recv_sem=z_recv.at[o],
            device_id={"outp": c}, device_id_type=MESH,
        )

    def begin(c):
        product(c)
        pair_copy(c).start()
        store_grads(c).start()

    def spread(c):
        pair_copy(c).wait_recv()
        summed = (pf[c, d] + xr[c].astype(f32)).astype(bf16)

        @pl.when(c != o)
        def _():
            zs[c] = summed
            spread_copy(c).start()

        @pl.when(c == o)
        def _():
            zr[o] = summed

    for p in range(per):
        await_grads(i, e, p)
    for copy in weights:
        copy.wait()
    for p in range(per):
        begin(i * per + p)
    for p in range(per):
        spread(i * per + p)

    def take_tokens():
        for s in range(1, n_outp):
            pltpu.make_async_remote_copy(
                src_ref=tk.at[outps[s], d], dst_ref=tk.at[outps[s], d],
                send_sem=t_send.at[0], recv_sem=t_recv.at[outps[s]],
                device_id={"depth": e}, device_id_type=MESH,
            ).wait_recv()
        onward = pltpu.make_async_remote_copy(
            src_ref=tk.at[:, d], dst_ref=tk.at[:, d], send_sem=f_send, recv_sem=f_recv,
            device_id={"depth": e}, device_id_type=MESH,
        )
        onward.start()
        pltpu.make_async_remote_copy(
            src_ref=tk.at[:, e], dst_ref=tk.at[:, e], send_sem=f_send, recv_sem=f_recv,
            device_id={"depth": e}, device_id_type=MESH,
        ).wait_recv()

        def step(t, carry):
            cols = pl.ds(pl.multiple_of(t * fw, fw), fw)
            turned[cols, :] = tk[:, :, :, cols].reshape(n_outp * 2 * rows, fw).T
            return carry
        lax.fori_loop(0, feats // fw, step, 0)
        result = pltpu.make_async_copy(turned, turned_out, out_sem.at[0])
        result.start()
        return onward, result

    later = [(s, p) for s in range(1, n_inp) for p in range(per)]
    onward = turned_copy = None
    for at, (s, p) in enumerate(later):
        if at == len(later) - 1:
            onward, turned_copy = take_tokens()
        for q in (d, e):
            await_grads(inps[s], q, p)
        begin(inps[s] * per + p)
        spread(inps[s] * per + p)

    for s in range(1, n_outp):
        pltpu.make_async_remote_copy(
            src_ref=zr.at[outps[s]], dst_ref=zr.at[outps[s]],
            send_sem=z_send.at[0], recv_sem=z_recv.at[outps[s]],
            device_id={"depth": e}, device_id_type=MESH,
        ).wait_recv()

    def total(t, carry):
        cols = pl.ds(pl.multiple_of(t * fw, fw), fw)
        acc = zr[0, :, cols].astype(f32)
        for c in range(1, n_outp):
            acc = acc + zr[c, :, cols].astype(f32)
        ov[:, cols] = acc.astype(bf16)
        return carry
    lax.fori_loop(0, feats // fw, total, 0)
    result = pltpu.make_async_copy(ov, out, out_sem.at[1])
    result.start()

    for copy in sends:
        copy.wait_send()
    onward.wait_send()
    for c in range(n_outp):
        pair_copy(c).wait_send()
        store_grads(c).wait()

        @pl.when(c != o)
        def _():
            spread_copy(c).wait_send()
    turned_copy.wait()
    result.wait()


def weight_grads(turned, grads, out_gate, out_up):
    left = turned[...]
    cw = width(out_gate.shape[1])
    for c in range(out_gate.shape[1] // cw):
        cols = slice(c * cw, (c + 1) * cw)
        out_gate[:, cols] = jnp.dot(left, grads[0, :, cols], preferred_element_type=f32).astype(bf16)
        out_up[:, cols] = jnp.dot(left, grads[1, :, cols], preferred_element_type=f32).astype(bf16)


def local(n_inp, n_outp, tokens, gate_pre, up_pre, grad_hidden, gate_weight, up_weight):
    rows, feats = tokens.shape
    trows, hid = gate_pre.shape
    half = hid // 2
    per = trows // rows
    every = n_outp * 2 * rows
    dma = pltpu.SemaphoreType.DMA
    anywhere = pl.BlockSpec(memory_space=pl.ANY)
    grad_tokens, grads, turned = pl.pallas_call(
        functools.partial(exchange, n_inp, n_outp),
        out_shape=(
            jax.ShapeDtypeStruct((rows, feats), bf16),
            jax.ShapeDtypeStruct((2, n_outp, 2, rows, half), bf16),
            jax.ShapeDtypeStruct((feats, every), bf16),
        ),
        in_specs=[anywhere] * 6,
        out_specs=(anywhere,) * 3,
        scratch_shapes=[
            pltpu.VMEM((trows, hid), bf16),
            pltpu.VMEM((trows, hid), bf16),
            pltpu.VMEM((trows, hid), bf16),
            pltpu.VMEM(gate_weight.shape, bf16),
            pltpu.VMEM(up_weight.shape, bf16),
            pltpu.VMEM((n_outp, 2, rows, feats), bf16),
            pltpu.VMEM((feats, every), bf16),
            pltpu.VMEM((2, n_outp, 2, rows, half), bf16),
            pltpu.VMEM((2, per, rows, half), bf16),
            pltpu.VMEM((n_outp, 2, rows, feats), f32),
            pltpu.VMEM((n_outp, 2, rows, feats), bf16),
            pltpu.VMEM((n_outp, rows, feats), bf16),
            pltpu.VMEM((n_outp, rows, feats), bf16),
            pltpu.VMEM((n_outp, rows, feats), bf16),
            pltpu.VMEM((rows, feats), bf16),
            dma((per, 3)), dma, dma((2,)),
            dma((n_outp,)), dma((n_outp,)), dma, dma,
            dma((n_inp, 2, per)), dma((n_inp, 2, per)),
            dma((n_outp,)), dma((n_outp,)),
            dma((n_outp,)), dma((n_outp,)),
            dma((n_outp,)), dma((2,)),
        ],
        compiler_params=pltpu.CompilerParams(
            collective_id=0, has_side_effects=True, vmem_limit_bytes=VMEM_BYTES
        ),
    )(tokens, gate_pre, up_pre, grad_hidden, gate_weight, up_weight)
    grads = grads.reshape(2, every, half)
    fw = width(feats)
    out_gate, out_up = pl.pallas_call(
        weight_grads,
        grid=(feats // fw,),
        out_shape=(jax.ShapeDtypeStruct((feats, half), bf16),) * 2,
        in_specs=[
            pl.BlockSpec((fw, every), lambda t: (t, 0)),
            pl.BlockSpec((2, every, half), lambda t: (0, 0, 0)),
        ],
        out_specs=(pl.BlockSpec((fw, half), lambda t: (t, 0)),) * 2,
        compiler_params=pltpu.CompilerParams(vmem_limit_bytes=VMEM_BYTES),
    )(turned, grads)
    return grad_tokens, out_gate, out_up


def solution(mesh):
    placed = (
        P(("groups", "depth", "outp"), "inp"),
        P(("groups", "depth", "inp"), "outp"),
        P(("groups", "depth", "inp"), "outp"),
        P(("groups", "depth", "inp"), "outp"),
        P("inp", ("outp", "depth")),
        P("inp", ("outp", "depth")),
    )
    return jax.shard_map(
        functools.partial(local, mesh.shape["inp"], mesh.shape["outp"]),
        mesh=mesh,
        in_specs=placed,
        out_specs=(
            P(("groups", "depth", "outp"), "inp"),
            P(("groups", "inp"), ("outp", "depth")),
            P(("groups", "inp"), ("outp", "depth")),
        ),
        check_vma=False,
    )
```

time: 337 us -> 101 us (0.30)
  the two profiles are of different devices: /device:TPU:0 before, /device:TPU:25 now
where the time goes in v1:
time: 101 us
  Pallas kernels  98.3 us (97%)
  local copies, waits for them, and re-layouts  1.72 us (2%)
    pallas_call x1, Pallas kernels, local(): pl.pallas_call(functools.partial(exchange, n_inp, n_outp), out_shape=(jax...  81.8 us
    pallas_call x1, Pallas kernels, local(): pl.pallas_call(weight_grads, grid=(feats // fw,), out_shape=(jax.ShapeDty...  16.4 us

profile of v1, /device:TPU:25, one launch (start us, length us, event | category | flops | bytes accessed | tf_op | source)
XLA Modules:
  0.0 100.7 jit_solution(5513447480389353920)
XLA Ops:
  0.6 81.8 %shard_map.85 = (bf16[64,2560]{1,0:T(8,128)(2,1)}, bf16[2,4,2,64,2048]{4,3,2,1,0:T(8,128)(2,1)}, bf16[2560,512]{1,0:T(8,128)(2,1)}) custom-call(bf16[64,2560]{1,0:T(8,128)(2,1)} %tokens.1, bf16[128,4096]{1,0:T(8,128)(2,1)} %gate.1, bf16[128,4096]{1,0:T(8,128)(2,1)} %up.1, bf16[128,4096]{1,0:T(8,128)(2,1)} %hidden.1, bf16[2560,2048]{1,0:T(8,128)(2,1)} %w_gate.1, ...), custom_call_target="tpu_custom_call" | custom-call | tf_op jit(solution)/shard_map/pallas_call | solution.py:265
  82.5 16.4 %shard_map.86 = (bf16[2560,2048]{1,0:T(8,128)(2,1)}, bf16[2560,2048]{1,0:T(8,128)(2,1)}) custom-call(bf16[2560,512]{1,0:T(8,128)(2,1)} %get-tuple-element.9.turned, bf16[2,512,2048]{2,1,0:T(8,128)(2,1)} %bitcast.1), custom_call_target="tpu_custom_call" | custom-call | tf_op jit(solution)/shard_map/pallas_call | solution.py:303
  98.9 1.7 %copy.10 = bf16[64,2560]{1,0:T(8,128)(2,1)} copy(bf16[64,2560]{1,0:T(8,128)(2,1)} %get-tuple-element.16) | data formatting | bytes 655360

commit v2 on v1

v2 whole, which is shorter than its diff:
```python
import functools

import jax
import jax.numpy as jnp
from jax import lax
from jax.experimental import pallas as pl
from jax.experimental.pallas import tpu as pltpu
from jax.sharding import PartitionSpec as P

MESH = pl.DeviceIdType.MESH
f32, bf16 = jnp.float32, jnp.bfloat16
VMEM_BYTES = 60 * 1024 * 1024


def width(extent):
    return 256 if extent % 256 == 0 else 128


def exchange(
    n_inp, n_outp,
    tokens, gate, up, hidden, w_gate, w_up,
    out, grads_out, turned_out, *rest,
):
    tails = rest[:n_outp]
    (
        gv, uv, hv, wg, wu, tk, turned, gr, sb, pf, pb, xr, zs, zr, ov,
        in_sem, own_sem, w_sem, t_send, t_recv, f_send, f_recv,
        g_send, g_recv, x_send, x_recv, z_send, z_recv, o_sem, out_sem, tail_sem,
    ) = rest[n_outp:]
    i, o, d = lax.axis_index("inp"), lax.axis_index("outp"), lax.axis_index("depth")
    e = 1 - d
    per, parts, rows = gate.shape[:3]
    half = gate.shape[3] // 2
    feats = tokens.shape[2]
    oi, op = o // per, lax.rem(o, per)
    inps = [lax.rem(i + s, n_inp) for s in range(n_inp)]
    outps = [lax.rem(o + s, n_outp) for s in range(n_outp)]
    last = parts - 1

    loads = [
        [
            pltpu.make_async_copy(src.at[:, q], dst.at[:, q], in_sem.at[q, k])
            for k, (src, dst) in enumerate(((gate, gv), (up, uv), (hidden, hv)))
        ]
        for q in range(parts)
    ]
    own = pltpu.make_async_copy(tokens, tk.at[oi, :, op, d], own_sem)
    weights = [
        pltpu.make_async_copy(w_gate, wg, w_sem.at[0]),
        pltpu.make_async_copy(w_up, wu, w_sem.at[1]),
    ]
    for copy in loads[0] + [own] + sum(loads[1:], []) + weights:
        copy.start()

    barrier = pltpu.get_barrier_semaphore()
    for s in range(n_inp):
        for side in ((e,) if s == 0 else (d, e)):
            pl.semaphore_signal(barrier, inc=1, device_id={"inp": inps[s], "depth": side}, device_id_type=MESH)
    for s in range(1, n_outp):
        pl.semaphore_signal(barrier, inc=1, device_id={"outp": outps[s]}, device_id_type=MESH)
    pl.semaphore_wait(barrier, 2 * n_inp - 1 + n_outp - 1)

    cw = width(half)

    def pointwise(q, side, store):
        def step(c, carry):
            from_cols = pl.ds(pl.multiple_of(side * half + c * cw, cw), cw)
            cols = pl.ds(pl.multiple_of(c * cw, cw), cw)
            for p in range(per):
                g = gv[p, q, :, from_cols].astype(f32)
                u = uv[p, q, :, from_cols].astype(f32)
                h = hv[p, q, :, from_cols].astype(f32)
                sig = 1.0 / (1.0 + jnp.exp(-g))
                hs = h * sig
                store(p, cols, (hs * u * (1.0 + g * (1.0 - sig))).astype(bf16), (hs * g).astype(bf16))
            return carry
        lax.fori_loop(0, half // cw, step, 0)

    def grad_copy(q, s, far, src):
        return pltpu.make_async_remote_copy(
            src_ref=src, dst_ref=gr.at[:, i, q, :, d],
            send_sem=g_send.at[s, far, q], recv_sem=g_recv.at[i, d, q],
            device_id={"inp": inps[s], "depth": e if far else d}, device_id_type=MESH,
        )

    sends = []
    for q in range(parts):
        for copy in loads[q]:
            copy.wait()

        def store_there(p, cols, a, b):
            sb[0, q, p, :, cols] = a
            sb[1, q, p, :, cols] = b

        def store_here(p, cols, a, b):
            gr[0, i, q, p, d, :, cols] = a
            gr[1, i, q, p, d, :, cols] = b

        pointwise(q, e, store_there)
        for s in list(range(1, n_inp)) + [0]:
            copy = grad_copy(q, s, 1, sb.at[:, q])
            copy.start()
            sends.append(copy)
        pointwise(q, d, store_here)
        for s in range(1, n_inp):
            copy = grad_copy(q, s, 0, gr.at[:, i, q, :, d])
            copy.start()
            sends.append(copy)
        if q == 0:
            own.wait()
            for s in range(1, n_outp):
                copy = pltpu.make_async_remote_copy(
                    src_ref=tk.at[oi, :, op, d], dst_ref=tk.at[oi, :, op, d],
                    send_sem=t_send.at[s], recv_sem=t_recv.at[o],
                    device_id={"outp": outps[s]}, device_id_type=MESH,
                )
                copy.start()
                sends.append(copy)

    def arrival(slot, send_sem, recv_sem):
        return pltpu.make_async_remote_copy(
            src_ref=slot, dst_ref=slot, send_sem=send_sem, recv_sem=recv_sem,
            device_id={"depth": e}, device_id_type=MESH,
        )

    def await_grads(j, side, q):
        arrival(gr.at[:, j, q, :, side], g_send.at[0, 0, 0], g_recv.at[j, side, q]).wait_recv()

    fw = width(feats)

    def product(j, first, count):
        chosen = pl.ds(first, count)
        left_gate = gr[0, j, chosen].reshape(count * per * 2 * rows, half)
        left_up = gr[1, j, chosen].reshape(count * per * 2 * rows, half)

        def step(t, carry):
            cols = pl.ds(pl.multiple_of(t * fw, fw), fw)
            contract = (((1,), (1,)), ((), ()))
            acc = lax.dot_general(left_gate, wg[cols, :], contract, preferred_element_type=f32)
            acc = acc + lax.dot_general(left_up, wu[cols, :], contract, preferred_element_type=f32)
            acc = acc.reshape(count, per, 2, rows, fw)
            pf[j, chosen, :, :, :, cols] = acc
            pb[j, chosen, :, :, :, cols] = acc.astype(bf16)
            return carry
        lax.fori_loop(0, feats // fw, step, 0)

    def pair_copy(j, q):
        return pltpu.make_async_remote_copy(
            src_ref=pb.at[j, q, :, e], dst_ref=xr.at[j, q], send_sem=x_send.at[j, q], recv_sem=x_recv.at[j, q],
            device_id={"depth": e}, device_id_type=MESH,
        )

    def store_grads(j, q):
        return pltpu.make_async_copy(gr.at[:, j, q], grads_out.at[:, j, q], o_sem.at[j, q])

    def spread_copy(j, q, p):
        c = j * per + p
        return pltpu.make_async_remote_copy(
            src_ref=zs.at[j, q, p], dst_ref=zr.at[q, o], send_sem=z_send.at[q, c], recv_sem=z_recv.at[q, o],
            device_id={"outp": c}, device_id_type=MESH,
        )

    def tail_copy(j, p, k):
        return pltpu.make_async_copy(zs.at[j, last, p], tails[k], tail_sem.at[k])

    def begin(j, first, count):
        product(j, first, count)
        for q in range(first, first + count):
            pair_copy(j, q).start()
        for q in range(first, first + count):
            store_grads(j, q).start()

    def spread(j, q):
        pair_copy(j, q).wait_recv()
        for p in range(per):
            c = j * per + p
            zs[j, q, p] = (pf[j, q, p, d] + xr[j, q, p].astype(f32)).astype(bf16)
            if q == last:
                for k in range(n_outp):
                    @pl.when(lax.rem(c - o + n_outp, n_outp) == k)
                    def _():
                        tail_copy(j, p, k).start()
            else:
                @pl.when(c != o)
                def _():
                    spread_copy(j, q, p).start()

                @pl.when(c == o)
                def _():
                    zr[q, o] = zs[j, q, p]

    for q in range(parts):
        await_grads(i, e, q)
    for copy in weights:
        copy.wait()
    begin(i, 0, parts)
    for q in range(parts):
        spread(i, q)

    def take_tokens():
        for s in range(1, n_outp):
            c = outps[s]
            arrival(tk.at[c // per, :, lax.rem(c, per), d], t_send.at[0], t_recv.at[c]).wait_recv()
        onward = pltpu.make_async_remote_copy(
            src_ref=tk.at[:, :, :, d], dst_ref=tk.at[:, :, :, d], send_sem=f_send, recv_sem=f_recv,
            device_id={"depth": e}, device_id_type=MESH,
        )
        onward.start()
        arrival(tk.at[:, :, :, e], f_send, f_recv).wait_recv()

        def step(t, carry):
            cols = pl.ds(pl.multiple_of(t * fw, fw), fw)
            turned[cols, :] = tk[:, :, :, :, :, cols].reshape(turned.shape[1], fw).T
            return carry
        lax.fori_loop(0, feats // fw, step, 0)
        result = pltpu.make_async_copy(turned, turned_out, out_sem.at[0])
        result.start()
        return onward, result

    later = [(s, q) for q in range(parts) for s in range(1, n_inp)]
    onward = turned_copy = None
    for at, (s, q) in enumerate(later):
        if at == len(later) - 1:
            onward, turned_copy = take_tokens()
        for side in (d, e):
            await_grads(inps[s], side, q)
        begin(inps[s], q, 1)
        spread(inps[s], q)

    for q in range(last):
        for s in range(1, n_outp):
            arrival(zr.at[q, outps[s]], z_send.at[0, 0], z_recv.at[q, outps[s]]).wait_recv()

        def total(t, carry):
            cols = pl.ds(pl.multiple_of(t * fw, fw), fw)
            acc = zr[q, 0, :, cols].astype(f32)
            for c in range(1, n_outp):
                acc = acc + zr[q, c, :, cols].astype(f32)
            ov[q, :, cols] = acc.astype(bf16)
            return carry
        lax.fori_loop(0, feats // fw, total, 0)
    results = [turned_copy]
    if last:
        results.append(pltpu.make_async_copy(ov, out, out_sem.at[1]))
        results[-1].start()

    for copy in sends:
        copy.wait_send()
    onward.wait_send()
    for j in range(n_inp):
        for q in range(parts):
            pair_copy(j, q).wait_send()
            store_grads(j, q).wait()
            for p in range(per if q != last else 0):
                @pl.when(j * per + p != o)
                def _():
                    spread_copy(j, q, p).wait_send()
    for k in range(n_outp):
        tail_copy(0, 0, k).wait()
    for copy in results:
        copy.wait()


def weight_grads(turned, grads, out_gate, out_up):
    left = turned[...]
    cw = width(out_gate.shape[1])
    for c in range(out_gate.shape[1] // cw):
        cols = slice(c * cw, (c + 1) * cw)
        out_gate[:, cols] = jnp.dot(left, grads[0, :, cols], preferred_element_type=f32).astype(bf16)
        out_up[:, cols] = jnp.dot(left, grads[1, :, cols], preferred_element_type=f32).astype(bf16)


def local(n_inp, n_outp, tokens, gate_pre, up_pre, grad_hidden, gate_weight, up_weight):
    block, feats = tokens.shape
    trows, hid = gate_pre.shape
    half = hid // 2
    per = trows // block
    parts = 2 if block % 32 == 0 else 1
    rows = block // parts
    spread_parts = max(parts - 1, 1)
    every = n_outp * 2 * block
    dma = pltpu.SemaphoreType.DMA
    anywhere = pl.BlockSpec(memory_space=pl.ANY)
    cut = (per, parts, rows, hid)
    done, grads, turned, *tails = pl.pallas_call(
        functools.partial(exchange, n_inp, n_outp),
        out_shape=(
            jax.ShapeDtypeStruct((spread_parts, rows, feats), bf16),
            jax.ShapeDtypeStruct((2, n_inp, parts, per, 2, rows, half), bf16),
            jax.ShapeDtypeStruct((feats, every), bf16),
        ) + (jax.ShapeDtypeStruct((rows, feats), bf16),) * n_outp,
        in_specs=[anywhere] * 6,
        out_specs=(anywhere,) * (3 + n_outp),
        scratch_shapes=[
            pltpu.VMEM(cut, bf16),
            pltpu.VMEM(cut, bf16),
            pltpu.VMEM(cut, bf16),
            pltpu.VMEM(gate_weight.shape, bf16),
            pltpu.VMEM(up_weight.shape, bf16),
            pltpu.VMEM((n_inp, parts, per, 2, rows, feats), bf16),
            pltpu.VMEM((feats, every), bf16),
            pltpu.VMEM((2, n_inp, parts, per, 2, rows, half), bf16),
            pltpu.VMEM((2, parts, per, rows, half), bf16),
            pltpu.VMEM((n_inp, parts, per, 2, rows, feats), f32),
            pltpu.VMEM((n_inp, parts, per, 2, rows, feats), bf16),
            pltpu.VMEM((n_inp, parts, per, rows, feats), bf16),
            pltpu.VMEM((n_inp, parts, per, rows, feats), bf16),
            pltpu.VMEM((spread_parts, n_outp, rows, feats), bf16),
            pltpu.VMEM((spread_parts, rows, feats), bf16),
            dma((parts, 3)), dma, dma((2,)),
            dma((n_outp,)), dma((n_outp,)), dma, dma,
            dma((n_inp, 2, parts)), dma((n_inp, 2, parts)),
            dma((n_inp, parts)), dma((n_inp, parts)),
            dma((spread_parts, n_outp)), dma((spread_parts, n_outp)),
            dma((n_inp, parts)), dma((2,)), dma((n_outp,)),
        ],
        compiler_params=pltpu.CompilerParams(
            collective_id=0, has_side_effects=True, vmem_limit_bytes=VMEM_BYTES
        ),
    )(
        tokens.reshape(parts, rows, feats),
        gate_pre.reshape(cut), up_pre.reshape(cut), grad_hidden.reshape(cut),
        gate_weight, up_weight,
    )

    total = tails[0].astype(f32)
    for k in range(1, n_outp):
        shift = [(c, (c + k) % n_outp) for c in range(n_outp)]
        total = total + lax.ppermute(tails[k], "outp", shift).astype(f32)
    total = total.astype(bf16)
    grad_tokens = jnp.concatenate([done.reshape(-1, feats), total]) if parts > 1 else total

    grads = grads.reshape(2, every, half)
    fw = 640 if feats % 640 == 0 else width(feats)
    out_gate, out_up = pl.pallas_call(
        weight_grads,
        grid=(feats // fw,),
        out_shape=(jax.ShapeDtypeStruct((feats, half), bf16),) * 2,
        in_specs=[
            pl.BlockSpec((fw, every), lambda t: (t, 0)),
            pl.BlockSpec((2, every, half), lambda t: (0, 0, 0)),
        ],
        out_specs=(pl.BlockSpec((fw, half), lambda t: (t, 0)),) * 2,
        compiler_params=pltpu.CompilerParams(vmem_limit_bytes=VMEM_BYTES),
        cost_estimate=pl.CostEstimate(
            flops=4 * every * feats * half, bytes_accessed=6 * feats * half, transcendentals=0
        ),
    )(turned, grads)
    return grad_tokens, out_gate, out_up


def solution(mesh):
    placed = (
        P(("groups", "depth", "outp"), "inp"),
        P(("groups", "depth", "inp"), "outp"),
        P(("groups", "depth", "inp"), "outp"),
        P(("groups", "depth", "inp"), "outp"),
        P("inp", ("outp", "depth")),
        P("inp", ("outp", "depth")),
    )
    return jax.shard_map(
        functools.partial(local, mesh.shape["inp"], mesh.shape["outp"]),
        mesh=mesh,
        in_specs=placed,
        out_specs=(
            P(("groups", "depth", "outp"), "inp"),
            P(("groups", "inp"), ("outp", "depth")),
            P(("groups", "inp"), ("outp", "depth")),
        ),
        check_vma=False,
    )
```

time: 101 us -> 84.6 us (0.84)
  the two profiles are of different devices: /device:TPU:25 before, /device:TPU:0 now
where the time goes in v2:
time: 84.6 us; the launch traced here: 84.3 us
  Pallas kernels  78.9 us (93%)
  starting transfers between devices  3.88 us (5%)
    pallas_call x1, Pallas kernels, local(): pl.pallas_call(functools.partial(exchange, n_inp, n_outp), out_shape=(jax...  62.4 us
    pallas_call x1, Pallas kernels, local(): pl.pallas_call(weight_grads, grid=(feats // fw,), out_shape=(jax.ShapeDty...  16.4 us
    ppermute x3, starting transfers between devices, local(): total = total + lax.ppermute(tails[k], 'outp', shift).astype(f32)  3.88 us
  transfers between devices with their start and end apart: 3, of which 0 were waited for; matrix products, arithmetic and copies ran while one was open for 0% of the time, Pallas kernels for 19%

profile of v2, /device:TPU:0, one launch (start us, length us, event | category | flops | bytes accessed | tf_op | source)
XLA Modules:
  0.0 84.3 jit_solution(1446678283424902753)
XLA Ops:
  0.6 62.4 %shard_map.85 = (bf16[1,32,2560]{2,1,0:T(8,128)(2,1)}, bf16[2,2,2,2,2,32,2048]{6,5,4,3,2,1,0:T(8,128)(2,1)}, bf16[2560,512]{1,0:T(8,128)(2,1)}, bf16[32,2560]{1,...) custom-call(bf16[2,32,2560]{2,1,0:T(8,128)(2,1)} %bitcast.9, ...), custom_call_target="tpu_custom_call" | custom-call | tf_op jit(solution)/shard_map/pallas_call | solution.py:285
  63.1 0.6 collective-permute-start
  63.7 1.6 %collective-permute-start.1 = (bf16[32,2560]{1,0:T(8,128)(2,1)}, bf16[32,2560]{1,0:T(8,128)(2,1)S(1)}, u32[]{:S(2)}, u32[]{:S(2)}) collective-permute-start(bf16[32,2560]{1,0:T(8,128)(2,1)} %get-tuple-element.15), channel_id=1, source_target_pairs={{0,4},{2,6},{4,0},{6,2},{1,5},{3,7},{5,1},{7,3},{8,12},{10,14},{12... | collective-permute-start | bytes 491528 | tf_op jit(solution)/shard_map/ppermute | solution.py:329
  65.3 1.7 %collective-permute-start.2 = (bf16[32,2560]{1,0:T(8,128)(2,1)}, bf16[32,2560]{1,0:T(8,128)(2,1)S(1)}, u32[]{:S(2)}, u32[]{:S(2)}) collective-permute-start(bf16[32,2560]{1,0:T(8,128)(2,1)} %get-tuple-element.16), channel_id=1, source_target_pairs={{0,6},{2,0},{4,2},{6,4},{1,7},{3,1},{5,3},{7,5},{8,14},{10,8},{12,... | collective-permute-start | bytes 491528 | tf_op jit(solution)/shard_map/ppermute | solution.py:329
  67.0 0.0 copy-start.1
  67.0 0.0 copy-start
  67.0 16.4 %shard_map.86 = (bf16[2560,2048]{1,0:T(8,128)(2,1)}, bf16[2560,2048]{1,0:T(8,128)(2,1)}) custom-call(bf16[2560,512]{1,0:T(8,128)(2,1)} %get-tuple-element.17.turned, bf16[2,512,2048]{2,1,0:T(8,128)(2,1)} %bitcast.11), custom_call_target="tpu_custom_call" | custom-call | flops 10737418240 | bytes 31457280 | tf_op jit(solution)/shard_map/pallas_call | solution.py:335
  83.4 0.0 collective-permute-done
  83.4 0.0 collective-permute-done.1
  83.4 0.0 collective-permute-done.2
  83.4 0.0 copy-done.1
  83.4 0.1 add_convert_fusion
  83.5 0.0 copy-done
  83.5 0.7 pad_maximum_fusion
Async XLA Ops:
  63.1 20.3 %collective-permute-start = (bf16[32,2560]{1,0:T(8,128)(2,1)}, bf16[32,2560]{1,0:T(8,128)(2,1)S(1)}, u32[]{:S(2)}, u32[]{:S(2)}) collective-permute-start(bf16[32,2560]{1,0:T(8,128)(2,1)} %get-tuple-element.14), channel_id=1, source_target_pairs={{0,2},{2,4},{4,6},{6,0},{1,3},{3,5},{5,7},{7,1},{8,10},{10,12},{12... | collective-permute-start | bytes 491528 | tf_op jit(solution)/shard_map/ppermute | solution.py:329
  63.7 19.7 %collective-permute-start.1 = (bf16[32,2560]{1,0:T(8,128)(2,1)}, bf16[32,2560]{1,0:T(8,128)(2,1)S(1)}, u32[]{:S(2)}, u32[]{:S(2)}) collective-permute-start(bf16[32,2560]{1,0:T(8,128)(2,1)} %get-tuple-element.15), channel_id=1, source_target_pairs={{0,4},{2,6},{4,0},{6,2},{1,5},{3,7},{5,1},{7,3},{8,12},{10,14},{12... | collective-permute-start | bytes 491528 | tf_op jit(solution)/shard_map/ppermute | solution.py:329
  65.3 18.1 %collective-permute-start.2 = (bf16[32,2560]{1,0:T(8,128)(2,1)}, bf16[32,2560]{1,0:T(8,128)(2,1)S(1)}, u32[]{:S(2)}, u32[]{:S(2)}) collective-permute-start(bf16[32,2560]{1,0:T(8,128)(2,1)} %get-tuple-element.16), channel_id=1, source_target_pairs={{0,6},{2,0},{4,2},{6,4},{1,7},{3,1},{5,3},{7,5},{8,14},{10,8},{12,... | collective-permute-start | bytes 491528 | tf_op jit(solution)/shard_map/ppermute | solution.py:329
  67.0 16.4 %copy-start.1 = (bf16[32,2560]{1,0:T(8,128)(2,1)S(1)}, bf16[32,2560]{1,0:T(8,128)(2,1)}, u32[]{:S(2)}) copy-start(bf16[32,2560]{1,0:T(8,128)(2,1)} %get-tuple-element.13) | copy-start | bytes 491524
  67.0 16.5 %copy-start = (bf16[1,32,2560]{2,1,0:T(8,128)(2,1)S(1)}, bf16[1,32,2560]{2,1,0:T(8,128)(2,1)}, u32[]{:S(2)}) copy-start(bf16[1,32,2560]{2,1,0:T(8,128)(2,1)} %get-tuple-element.12) | copy-start | bytes 491524

commit v3 on v2

--- a/solution.py
+++ b/solution.py
@@ -10,6 +10,7 @@
 MESH = pl.DeviceIdType.MESH
 f32, bf16 = jnp.float32, jnp.bfloat16
 VMEM_BYTES = 60 * 1024 * 1024
+PIECES = 2
 
 
 def width(extent):
@@ -36,6 +37,7 @@
     inps = [lax.rem(i + s, n_inp) for s in range(n_inp)]
     outps = [lax.rem(o + s, n_outp) for s in range(n_outp)]
     last = parts - 1
+    piece = half // PIECES
 
     loads = [
         [
@@ -58,11 +60,10 @@
             pl.semaphore_signal(barrier, inc=1, device_id={"inp": inps[s], "depth": side}, device_id_type=MESH)
     for s in range(1, n_outp):
         pl.semaphore_signal(barrier, inc=1, device_id={"outp": outps[s]}, device_id_type=MESH)
-    pl.semaphore_wait(barrier, 2 * n_inp - 1 + n_outp - 1)
-
-    cw = width(half)
-
-    def pointwise(q, side, store):
+
+    cw = width(piece)
+
+    def pointwise(q, side, store, begin, end):
         def step(c, carry):
             from_cols = pl.ds(pl.multiple_of(side * half + c * cw, cw), cw)
             cols = pl.ds(pl.multiple_of(c * cw, cw), cw)
@@ -74,12 +75,20 @@
                 hs = h * sig
                 store(p, cols, (hs * u * (1.0 + g * (1.0 - sig))).astype(bf16), (hs * g).astype(bf16))
             return carry
-        lax.fori_loop(0, half // cw, step, 0)
-
-    def grad_copy(q, s, far, src):
+        lax.fori_loop(begin // cw, end // cw, step, 0)
+
+    def spans(q):
+        if q == last:
+            return [(k * piece, (k + 1) * piece, last + k) for k in range(PIECES)]
+        return [(0, half, q)]
+
+    def grad_copy(q, s, far, span):
+        begin, end, sem = span
+        cols = pl.ds(begin, end - begin)
+        slot = gr.at[:, i, q, :, d, :, cols]
         return pltpu.make_async_remote_copy(
-            src_ref=src, dst_ref=gr.at[:, i, q, :, d],
-            send_sem=g_send.at[s, far, q], recv_sem=g_recv.at[i, d, q],
+            src_ref=sb.at[:, q, :, :, cols] if far else slot, dst_ref=slot,
+            send_sem=g_send.at[s, far, sem], recv_sem=g_recv.at[i, d, sem],
             device_id={"inp": inps[s], "depth": e if far else d}, device_id_type=MESH,
         )
 
@@ -96,16 +105,19 @@
             gr[0, i, q, p, d, :, cols] = a
             gr[1, i, q, p, d, :, cols] = b
 
-        pointwise(q, e, store_there)
-        for s in list(range(1, n_inp)) + [0]:
-            copy = grad_copy(q, s, 1, sb.at[:, q])
-            copy.start()
-            sends.append(copy)
-        pointwise(q, d, store_here)
-        for s in range(1, n_inp):
-            copy = grad_copy(q, s, 0, gr.at[:, i, q, :, d])
-            copy.start()
-            sends.append(copy)
+        for span in spans(q):
+            pointwise(q, e, store_there, *span[:2])
+            if not sends:
+                pl.semaphore_wait(barrier, 2 * n_inp - 1 + n_outp - 1)
+            for s in list(range(1, n_inp)) + [0]:
+                copy = grad_copy(q, s, 1, span)
+                copy.start()
+                sends.append(copy)
+            pointwise(q, d, store_here, *span[:2])
+            for s in range(1, n_inp):
+                copy = grad_copy(q, s, 0, span)
+                copy.start()
+                sends.append(copy)
         if q == 0:
             own.wait()
             for s in range(1, n_outp):
@@ -123,24 +135,29 @@
             device_id={"depth": e}, device_id_type=MESH,
         )
 
-    def await_grads(j, side, q):
-        arrival(gr.at[:, j, q, :, side], g_send.at[0, 0, 0], g_recv.at[j, side, q]).wait_recv()
+    def await_grads(j, side, q, span):
+        begin, end, sem = span
+        slot = gr.at[:, j, q, :, side, :, pl.ds(begin, end - begin)]
+        arrival(slot, g_send.at[0, 0, 0], g_recv.at[j, side, sem]).wait_recv()
 
     fw = width(feats)
 
-    def product(j, first, count):
-        chosen = pl.ds(first, count)
-        left_gate = gr[0, j, chosen].reshape(count * per * 2 * rows, half)
-        left_up = gr[1, j, chosen].reshape(count * per * 2 * rows, half)
+    def product(j, first, count, begin, end):
+        chosen, depth = pl.ds(first, count), pl.ds(begin, end - begin)
+        left_gate = gr[0, j, chosen, :, :, :, depth].reshape(count * per * 2 * rows, end - begin)
+        left_up = gr[1, j, chosen, :, :, :, depth].reshape(count * per * 2 * rows, end - begin)
 
         def step(t, carry):
             cols = pl.ds(pl.multiple_of(t * fw, fw), fw)
             contract = (((1,), (1,)), ((), ()))
-            acc = lax.dot_general(left_gate, wg[cols, :], contract, preferred_element_type=f32)
-            acc = acc + lax.dot_general(left_up, wu[cols, :], contract, preferred_element_type=f32)
+            acc = lax.dot_general(left_gate, wg[cols, depth], contract, preferred_element_type=f32)
+            acc = acc + lax.dot_general(left_up, wu[cols, depth], contract, preferred_element_type=f32)
             acc = acc.reshape(count, per, 2, rows, fw)
+            if begin > 0:
+                acc = acc + pf[j, chosen, :, :, :, cols]
             pf[j, chosen, :, :, :, cols] = acc
-            pb[j, chosen, :, :, :, cols] = acc.astype(bf16)
+            if end == half:
+                pb[j, chosen, :, :, :, cols] = acc.astype(bf16)
             return carry
         lax.fori_loop(0, feats // fw, step, 0)
 
@@ -164,7 +181,6 @@
         return pltpu.make_async_copy(zs.at[j, last, p], tails[k], tail_sem.at[k])
 
     def begin(j, first, count):
-        product(j, first, count)
         for q in range(first, first + count):
             pair_copy(j, q).start()
         for q in range(first, first + count):
@@ -190,9 +206,11 @@
                     zr[q, o] = zs[j, q, p]
 
     for q in range(parts):
-        await_grads(i, e, q)
+        for span in spans(q):
+            await_grads(i, e, q, span)
     for copy in weights:
         copy.wait()
+    product(i, 0, parts, 0, half)
     begin(i, 0, parts)
     for q in range(parts):
         spread(i, q)
@@ -206,6 +224,9 @@
             device_id={"depth": e}, device_id_type=MESH,
         )
         onward.start()
+        return onward
+
+    def turn_tokens():
         arrival(tk.at[:, :, :, e], f_send, f_recv).wait_recv()
 
         def step(t, carry):
@@ -215,16 +236,20 @@
         lax.fori_loop(0, feats // fw, step, 0)
         result = pltpu.make_async_copy(turned, turned_out, out_sem.at[0])
         result.start()
-        return onward, result
+        return result
 
     later = [(s, q) for q in range(parts) for s in range(1, n_inp)]
     onward = turned_copy = None
     for at, (s, q) in enumerate(later):
         if at == len(later) - 1:
-            onward, turned_copy = take_tokens()
-        for side in (d, e):
-            await_grads(inps[s], side, q)
+            onward = take_tokens()
+        for span in spans(q):
+            for side in (d, e):
+                await_grads(inps[s], side, q, span)
+            product(inps[s], q, 1, span[0], span[1])
         begin(inps[s], q, 1)
+        if at == len(later) - 1:
+            turned_copy = turn_tokens()
         spread(inps[s], q)
 
     for q in range(last):
@@ -262,12 +287,12 @@
 
 
 def weight_grads(turned, grads, out_gate, out_up):
-    left = turned[...]
-    cw = width(out_gate.shape[1])
-    for c in range(out_gate.shape[1] // cw):
-        cols = slice(c * cw, (c + 1) * cw)
-        out_gate[:, cols] = jnp.dot(left, grads[0, :, cols], preferred_element_type=f32).astype(bf16)
-        out_up[:, cols] = jnp.dot(left, grads[1, :, cols], preferred_element_type=f32).astype(bf16)
+    feats = turned.shape[0]
+    tall = 512 if feats % 512 == 0 else feats
+    for r in range(feats // tall):
+        at = slice(r * tall, (r + 1) * tall)
+        out_gate[at, :] = jnp.dot(turned[at, :], grads[0], preferred_element_type=f32).astype(bf16)
+        out_up[at, :] = jnp.dot(turned[at, :], grads[1], preferred_element_type=f32).astype(bf16)
 
 
 def local(n_inp, n_outp, tokens, gate_pre, up_pre, grad_hidden, gate_weight, up_weight):
@@ -309,7 +334,7 @@
             pltpu.VMEM((spread_parts, rows, feats), bf16),
             dma((parts, 3)), dma, dma((2,)),
             dma((n_outp,)), dma((n_outp,)), dma, dma,
-            dma((n_inp, 2, parts)), dma((n_inp, 2, parts)),
+            dma((n_inp, 2, parts - 1 + PIECES)), dma((n_inp, 2, parts - 1 + PIECES)),
             dma((n_inp, parts)), dma((n_inp, parts)),
             dma((spread_parts, n_outp)), dma((spread_parts, n_outp)),
             dma((n_inp, parts)), dma((2,)), dma((n_outp,)),
@@ -331,16 +356,16 @@
     grad_tokens = jnp.concatenate([done.reshape(-1, feats), total]) if parts > 1 else total
 
     grads = grads.reshape(2, every, half)
-    fw = 640 if feats % 640 == 0 else width(feats)
+    cw = 512 if half % 512 == 0 else width(half)
     out_gate, out_up = pl.pallas_call(
         weight_grads,
-        grid=(feats // fw,),
+        grid=(half // cw,),
         out_shape=(jax.ShapeDtypeStruct((feats, half), bf16),) * 2,
         in_specs=[
-            pl.BlockSpec((fw, every), lambda t: (t, 0)),
-            pl.BlockSpec((2, every, half), lambda t: (0, 0, 0)),
+            pl.BlockSpec((feats, every), lambda t: (0, 0)),
+            pl.BlockSpec((2, every, cw), lambda t: (0, 0, t)),
         ],
-        out_specs=(pl.BlockSpec((fw, half), lambda t: (t, 0)),) * 2,
+        out_specs=(pl.BlockSpec((feats, cw), lambda t: (0, t)),) * 2,
         compiler_params=pltpu.CompilerParams(vmem_limit_bytes=VMEM_BYTES),
         cost_estimate=pl.CostEstimate(
             flops=4 * every * feats * half, bytes_accessed=6 * feats * half, transcendentals=0

time: 84.6 us -> 81.8 us (0.967)
  Pallas kernels: 78.9 us -> 76.2 us
    pallas_call x1, Pallas kernels: 62.4 us -> 60.4 us  [local(): pl.pallas_call(functools.partial(exchange, n_inp, n_outp), out_shape=(jax...]
where the time goes in v3:
time: 81.8 us; the launch traced here: 81.6 us
  Pallas kernels  76.2 us (93%)
  starting transfers between devices  3.94 us (5%)
  other arithmetic  0.83 us (1%)
    pallas_call x1, Pallas kernels, local(): pl.pallas_call(functools.partial(exchange, n_inp, n_outp), out_shape=(jax...  60.4 us
    pallas_call x1, Pallas kernels, local(): pl.pallas_call(weight_grads, grid=(half // cw,), out_shape=(jax.ShapeDtyp...  15.8 us
    ppermute x3, starting transfers between devices, local(): total = total + lax.ppermute(tails[k], 'outp', shift).astype(f32)  3.94 us
  transfers between devices with their start and end apart: 3, of which 0 were waited for; matrix products, arithmetic and copies ran while one was open for 0% of the time, Pallas kernels for 19%

profile of v3, /device:TPU:0, one launch (start us, length us, event | category | flops | bytes accessed | tf_op | source)
XLA Modules:
  0.0 81.6 jit_solution(17372572324155110751)
XLA Ops:
  0.6 60.4 %shard_map.85 = (bf16[1,32,2560]{2,1,0:T(8,128)(2,1)}, bf16[2,2,2,2,2,32,2048]{6,5,4,3,2,1,0:T(8,128)(2,1)}, bf16[2560,512]{1,0:T(8,128)(2,1)}, bf16[32,2560]{1,...) custom-call(bf16[2,32,2560]{2,1,0:T(8,128)(2,1)} %bitcast.9, ...), custom_call_target="tpu_custom_call" | custom-call | tf_op jit(solution)/shard_map/pallas_call | solution.py:310
  61.0 0.6 collective-permute-start
  61.6 1.9 %collective-permute-start.1 = (bf16[32,2560]{1,0:T(8,128)(2,1)}, bf16[32,2560]{1,0:T(8,128)(2,1)S(1)}, u32[]{:S(2)}, u32[]{:S(2)}) collective-permute-start(bf16[32,2560]{1,0:T(8,128)(2,1)} %get-tuple-element.15), channel_id=1, source_target_pairs={{0,4},{2,6},{4,0},{6,2},{1,5},{3,7},{5,1},{7,3},{8,12},{10,14},{12... | collective-permute-start | bytes 491528 | tf_op jit(solution)/shard_map/ppermute | solution.py:354
  63.6 1.4 %collective-permute-start.2 = (bf16[32,2560]{1,0:T(8,128)(2,1)}, bf16[32,2560]{1,0:T(8,128)(2,1)S(1)}, u32[]{:S(2)}, u32[]{:S(2)}) collective-permute-start(bf16[32,2560]{1,0:T(8,128)(2,1)} %get-tuple-element.16), channel_id=1, source_target_pairs={{0,6},{2,0},{4,2},{6,4},{1,7},{3,1},{5,3},{7,5},{8,14},{10,8},{12,... | collective-permute-start | bytes 491528 | tf_op jit(solution)/shard_map/ppermute | solution.py:354
  64.9 0.0 copy-start.1
  64.9 0.0 copy-start
  64.9 15.8 %shard_map.86 = (bf16[2560,2048]{1,0:T(8,128)(2,1)}, bf16[2560,2048]{1,0:T(8,128)(2,1)}) custom-call(bf16[2560,512]{1,0:T(8,128)(2,1)} %get-tuple-element.17.turned, bf16[2,512,2048]{2,1,0:T(8,128)(2,1)} %bitcast.11), custom_call_target="tpu_custom_call" | custom-call | flops 10737418240 | bytes 31457280 | tf_op jit(solution)/shard_map/pallas_call | solution.py:360
  80.8 0.0 collective-permute-done
  80.8 0.0 collective-permute-done.1
  80.8 0.0 collective-permute-done.2
  80.8 0.0 copy-done.1
  80.8 0.1 add_convert_fusion
  80.9 0.0 copy-done
  80.9 0.7 pad_maximum_fusion
Async XLA Ops:
  61.0 19.8 %collective-permute-start = (bf16[32,2560]{1,0:T(8,128)(2,1)}, bf16[32,2560]{1,0:T(8,128)(2,1)S(1)}, u32[]{:S(2)}, u32[]{:S(2)}) collective-permute-start(bf16[32,2560]{1,0:T(8,128)(2,1)} %get-tuple-element.14), channel_id=1, source_target_pairs={{0,2},{2,4},{4,6},{6,0},{1,3},{3,5},{5,7},{7,1},{8,10},{10,12},{12... | collective-permute-start | bytes 491528 | tf_op jit(solution)/shard_map/ppermute | solution.py:354
  61.6 19.1 %collective-permute-start.1 = (bf16[32,2560]{1,0:T(8,128)(2,1)}, bf16[32,2560]{1,0:T(8,128)(2,1)S(1)}, u32[]{:S(2)}, u32[]{:S(2)}) collective-permute-start(bf16[32,2560]{1,0:T(8,128)(2,1)} %get-tuple-element.15), channel_id=1, source_target_pairs={{0,4},{2,6},{4,0},{6,2},{1,5},{3,7},{5,1},{7,3},{8,12},{10,14},{12... | collective-permute-start | bytes 491528 | tf_op jit(solution)/shard_map/ppermute | solution.py:354
  63.6 17.2 %collective-permute-start.2 = (bf16[32,2560]{1,0:T(8,128)(2,1)}, bf16[32,2560]{1,0:T(8,128)(2,1)S(1)}, u32[]{:S(2)}, u32[]{:S(2)}) collective-permute-start(bf16[32,2560]{1,0:T(8,128)(2,1)} %get-tuple-element.16), channel_id=1, source_target_pairs={{0,6},{2,0},{4,2},{6,4},{1,7},{3,1},{5,3},{7,5},{8,14},{10,8},{12,... | collective-permute-start | bytes 491528 | tf_op jit(solution)/shard_map/ppermute | solution.py:354
  64.9 15.8 %copy-start.1 = (bf16[32,2560]{1,0:T(8,128)(2,1)S(1)}, bf16[32,2560]{1,0:T(8,128)(2,1)}, u32[]{:S(2)}) copy-start(bf16[32,2560]{1,0:T(8,128)(2,1)} %get-tuple-element.13) | copy-start | bytes 491524
  64.9 15.9 %copy-start = (bf16[1,32,2560]{2,1,0:T(8,128)(2,1)S(1)}, bf16[1,32,2560]{2,1,0:T(8,128)(2,1)}, u32[]{:S(2)}) copy-start(bf16[1,32,2560]{2,1,0:T(8,128)(2,1)} %get-tuple-element.12) | copy-start | bytes 491524
